TPU v7x, 32 devices: a whole 2x2x4 slice. The times are simulated.
32 devices in a mesh: groups: 2 (over x), hid: 16 (over z, y, core).
Axes of the slice: x: 2, y: 2, z: 4, core: 2. Of those that a mesh axis runs over, the one named last changes fastest.
Arguments:
- gate_pre: bfloat16 [1024, 49152], P('groups', 'hid'), parts along dimension 0, may hold values from -6 to 6
- up_pre: bfloat16 [1024, 49152], P('groups', 'hid'), parts along dimension 0, may hold values from -7 to 7
- down_weight: bfloat16 [49152, 8192], P('hid'), may hold values from -1 to 1
- residual: bfloat16 [1024, 8192], P('groups', 'hid'), parts along dimension 0, may hold values from -38 to 38
- norm_gain: bfloat16 [8192], P('hid'), may hold values from 0.5 to 1.5
Outputs:
- stream: bfloat16 [1024, 8192], P('groups', 'hid'), parts along dimension 0
- normed: bfloat16 [1024, 8192], P('groups', 'hid'), parts along dimension 0
There are 2 independent parts, one for each index of `groups`. A program takes and returns all parts, laid end to end along the dimension named above; an argument that names none is the same for every part. Nothing has to cross between parts.
All inputs are finite; a program needn't handle non-finite values.
Results may differ from a plain program's by a relative error of at most 0.0031.
Values may be sent and summed in bfloat16 or wider, within the bound.
A program may use at most 192 MiB of HBM per device.

v0:
```python
import jax
import jax.numpy as jnp
from jax import lax
from jax.sharding import PartitionSpec as P


def finish(combined, gain_values, mean_square):
    stream = combined.astype(jnp.bfloat16)
    normed = (combined * lax.rsqrt(mean_square + 1e-05) * gain_values.astype(jnp.float32)).astype(
        jnp.bfloat16
    )
    return (stream, normed)


def body(gate_pre, up_pre, down_weight, residual, norm_gain):
    hidden = (jax.nn.silu(gate_pre.astype(jnp.float32)) * up_pre.astype(jnp.float32)).astype(
        jnp.bfloat16
    )
    summed = lax.psum_scatter(
        lax.dot_general(
            down_weight, hidden, (((0,), (1,)), ((), ())), preferred_element_type=jnp.float32
        ),
        "hid",
        scatter_dimension=0,
        tiled=True,
    )
    combined = residual.astype(jnp.float32) + summed.T
    squares = jnp.sum(combined * combined, axis=1, keepdims=True)
    mean_square = lax.psum(squares, "hid") / down_weight.shape[1]
    return finish(combined, norm_gain, mean_square)


def solution(mesh):
    return jax.shard_map(
        body,
        mesh=mesh,
        in_specs=(
            P("groups", "hid"),
            P("groups", "hid"),
            P("hid", None),
            P("groups", "hid"),
            P("hid"),
        ),
        out_specs=(P("groups", "hid"), P("groups", "hid")),
        check_vma=False,
    )
```

profile of v0, /device:TPU:0, one launch (start us, length us, event | category | flops | bytes accessed | tf_op | source)
XLA Modules:
  0.0 267.8 jit_solution(9561831269386114868)
XLA Ops:
  7.2 0.0 reduce-scatter.2.cloned.1.call-start
  7.2 37.0 %convolution_bitcast_fusion = f32[8192,512]{0,1:T(8,128)} fusion(bf16[3072,8192]{1,0:T(8,128)(2,1)} %param.7, bf16[512,3072]{1,0:T(8,128)(2,1)} %param.6, bf16[512,3072]{1,0:T(8,128)(2,1)} %param.5), kind=kOutput, calls=%fused_computation | convolution fusion | flops 25782386688 | bytes 73400320 | tf_op jit(solution)/shard_map/dot_general | solution.py:20
  44.2 0.0 copy-start.1
  44.2 0.0 copy-start
  44.2 0.0 reduce-scatter.2.cloned.1.call-update
  44.2 0.7 copy-done.1
  44.9 180.7 %reduce-scatter.2.cloned.1.call-done = f32[512,512]{0,1:T(8,128)} async-done(((f32[8192,512]{0,1:T(8,128)}), f32[512,512]{0,1:T(8,128)}) %reduce-scatter.2.cloned.1.call-update) | async-done | bytes 1048592 | tf_op jit(solution)/shard_map/reduce_scatter | solution.py:19
  225.6 0.0 copy-done
  225.6 1.4 multiply_reduce_fusion
  227.0 31.5 %psum.7 = f32[512,1]{0,1:T(1,128)S(1)} all-reduce(f32[512,1]{0,1:T(1,128)S(1)} %bitcast.14), channel_id=1, replica_groups=mesh['groups'=2,'hid'=16] {'hid'}, use_global_device_ids=true, to_apply=%region_2.3 | all-reduce | flops 512 | bytes 4096 | tf_op jit(solution)/shard_map/psum | solution.py:29
  258.6 2.4 multiply_convert_fusion
  (2 shorter events, 0.0 us)
Async XLA Ops:
  7.2 218.4 %reduce-scatter.2.cloned.1.call-start = ((), (), s32[]{:S(2)}) async-start(), calls=%async_computation.1 | async-start | bytes 17825792 | tf_op jit(solution)/shard_map/reduce_scatter | solution.py:19
  44.2 0.7 copy-start.1
  44.2 181.4 %copy-start = (bf16[512,512]{1,0:T(8,128)(2,1)S(1)}, bf16[512,512]{1,0:T(8,128)(2,1)}, u32[]{:S(2)}) copy-start(bf16[512,512]{1,0:T(8,128)(2,1)} %param.8) | copy-start | bytes 1572868
Sparse Core Ops, SparseCore 0:
  44.3 181.2 reduce-scatter.1
where the time goes:
time: 268 us
  waiting for transfers between devices  181 us (68%)
  matrix products  37 us (14%)
  blocking collectives  31.5 us (12%)
  between operations  14 us (5%)
  other arithmetic  3.82 us (1%)
    reduce_scatter x1, waiting for transfers between devices, body(): lax.psum_scatter(lax.dot_general(down_weight, hidden, (((0,), (1,)), ((),...  181 us
    dot_general x1, matrix products, body(): lax.dot_general(down_weight, hidden, (((0,), (1,)), ((), ())), preferred_...  37 us
    psum x1, blocking collectives, body(): mean_square = lax.psum(squares, 'hid') / down_weight.shape[1]  31.5 us
  transfers between devices with their start and end apart: 1, of which 1 were waited for; matrix products, arithmetic and copies ran while one was open for 0% of the time, Pallas kernels for 0%

commit v1 on v0

v1 whole, which is shorter than its diff:
```python
import functools

import jax
import jax.numpy as jnp
from jax import lax
from jax.experimental import pallas as pl
from jax.experimental.pallas import tpu as pltpu
from jax.sharding import PartitionSpec as P

MESH = pl.DeviceIdType.MESH
SLOTS = 3
LOADS = 8


def kernel(
    n, total_features,
    gate_hbm, up_hbm, weight_hbm, residual_ref, gain_ref,
    stream_ref, normed_ref,
    gate, up, hidden, weights, acc, combined,
    send_c, recv_c, send_y, recv_y, send_z, recv_z, stats,
    load_sem, weight_sem, c_send_sem, c_recv_sem, y_send_sem, y_recv_sem,
    z_send_sem, z_recv_sem, s_send_sem, s_recv_sem,
):
    nz = n // 4
    tokens, feats = residual_ref.shape
    me = lax.axis_index("hid")
    core = lax.rem(me, 2)
    row = lax.rem(lax.div(me, 2), 2)
    layer = lax.div(me, 4)
    sibling = me + 1 - 2 * core
    across = me + 2 - 4 * row
    steps = 4 * nz

    barrier = pltpu.get_barrier_semaphore()

    @pl.loop(1, n)
    def _(k):
        pl.semaphore_signal(
            barrier, inc=1, device_id={"hid": lax.rem(me + k, n)}, device_id_type=MESH
        )

    load_rows = tokens // LOADS

    def input_copies(i):
        rows = pl.ds(i * load_rows, load_rows)
        return (
            pltpu.make_async_copy(gate_hbm.at[rows], gate.at[rows], load_sem.at[0, i]),
            pltpu.make_async_copy(up_hbm.at[rows], up.at[rows], load_sem.at[1, i]),
        )

    def split(s):
        phase = s // (2 * nz)
        j = (s // 2) % nz
        own = s % 2
        return phase, j, own

    def weight_copy(s):
        phase, j, own = split(s)
        dest_z = lax.rem(layer + 1 + j, nz)
        dest_y = jnp.where(phase == 0, 1 - row, row)
        dest_c = jnp.where(own == 1, core, 1 - core)
        dest = (dest_z * 2 + dest_y) * 2 + dest_c
        slot = lax.rem(s, SLOTS)
        columns = pl.ds(pl.multiple_of(dest * feats, feats), feats)
        return pltpu.make_async_copy(
            weight_hbm.at[:, columns], weights.at[slot], weight_sem.at[slot]
        )

    for i in range(LOADS):
        for copy in input_copies(i):
            copy.start()
    for s in range(SLOTS - 1):
        weight_copy(jnp.int32(s)).start()

    for i in range(LOADS):
        for copy in input_copies(i):
            copy.wait()

        @pl.loop(0, load_rows // 16)
        def _(r):
            rows = pl.ds(pl.multiple_of(i * load_rows + r * 16, 16), 16)
            half = gate[rows, :].astype(jnp.float32) * 0.5
            silu = half + half * jnp.tanh(half)
            hidden[rows, :] = (silu * up[rows, :].astype(jnp.float32)).astype(jnp.bfloat16)

    pl.semaphore_wait(barrier, n - 1)

    def c_copy(i):
        return pltpu.make_async_remote_copy(
            src_ref=send_c.at[i], dst_ref=recv_c.at[i],
            send_sem=c_send_sem.at[i], recv_sem=c_recv_sem.at[i],
            device_id={"hid": sibling}, device_id_type=MESH,
        )

    def y_copy(j):
        return pltpu.make_async_remote_copy(
            src_ref=send_y.at[j], dst_ref=recv_y.at[j],
            send_sem=y_send_sem.at[j], recv_sem=y_recv_sem.at[j],
            device_id={"hid": across}, device_id_type=MESH,
        )

    def z_copy(j):
        return pltpu.make_async_remote_copy(
            src_ref=send_z.at[j], dst_ref=recv_z.at[j],
            send_sem=z_send_sem.at[j], recv_sem=z_recv_sem.at[j],
            device_id={"hid": lax.rem(me + 4 * (1 + j), n)}, device_id_type=MESH,
        )

    chunk = 64

    def by_rows(work):
        @pl.loop(0, tokens // chunk)
        def _(r):
            work(pl.ds(pl.multiple_of(r * chunk, chunk), chunk))

    f32 = jnp.float32

    @pl.loop(0, steps)
    def _(s):
        phase, j, own = split(s)
        weight_copy(s).wait()

        @pl.when(s + SLOTS - 1 < steps)
        def _():
            weight_copy(s + SLOTS - 1).start()

        acc[...] = jnp.dot(
            hidden[...], weights[lax.rem(s, SLOTS)], preferred_element_type=f32
        )
        at = phase * nz + j

        @pl.when(own == 0)
        def _():
            def work(rows):
                send_c[at, rows, :] = acc[rows, :].astype(jnp.bfloat16)

            by_rows(work)
            c_copy(at).start()

        @pl.when(own == 1)
        def _():
            c_copy(at).wait_recv()

            @pl.when(phase == 0)
            def _():
                def work(rows):
                    send_y[j, rows, :] = (
                        acc[rows, :] + recv_c[at, rows, :].astype(f32)
                    ).astype(jnp.bfloat16)

                by_rows(work)
                y_copy(j).start()

            @pl.when(phase == 1)
            def _():
                y_copy(j).wait_recv()

                @pl.when(j < nz - 1)
                def _():
                    def work(rows):
                        send_z[j, rows, :] = (
                            acc[rows, :] + recv_c[at, rows, :].astype(f32)
                            + recv_y[j, rows, :].astype(f32)
                        ).astype(jnp.bfloat16)

                    by_rows(work)
                    z_copy(j).start()

                @pl.when(j == nz - 1)
                def _():
                    def work(rows):
                        combined[rows, :] = (
                            acc[rows, :] + recv_c[at, rows, :].astype(f32)
                            + recv_y[j, rows, :].astype(f32)
                            + residual_ref[rows, :].astype(f32)
                        )

                    by_rows(work)

    @pl.loop(0, nz - 1)
    def _(j):
        z_copy(j).wait_recv()

        def work(rows):
            combined[rows, :] += recv_z[j, rows, :].astype(f32)

        by_rows(work)

    block = 128

    @pl.loop(0, tokens // block)
    def _(r):
        rows = pl.ds(pl.multiple_of(r * block, block), block)
        values = combined[rows, :]
        stream_ref[rows, :] = values.astype(jnp.bfloat16)
        squares = values * values
        folded = squares[:, 0:128]
        for f in range(1, feats // 128):
            folded += squares[:, f * 128:(f + 1) * 128]
        sums = jnp.sum(folded.T, axis=0, keepdims=True)
        stats[0, :, rows] = jnp.broadcast_to(sums, (8, block))

    def s_copy(k):
        return pltpu.make_async_remote_copy(
            src_ref=stats.at[0], dst_ref=stats.at[k],
            send_sem=s_send_sem.at[k], recv_sem=s_recv_sem.at[k],
            device_id={"hid": lax.rem(me + k, n)}, device_id_type=MESH,
        )

    @pl.loop(1, n)
    def _(k):
        s_copy(k).start()

    @pl.loop(1, n)
    def _(k):
        s_copy(k).wait_recv()

    gain = gain_ref[...].astype(f32)

    @pl.loop(0, tokens // block)
    def _(r):
        rows = pl.ds(pl.multiple_of(r * block, block), block)
        whole = stats[0, :, rows]
        for k in range(1, n):
            whole += stats[k, :, rows]
        scale = lax.rsqrt(whole / total_features + 1e-05)
        scale = jnp.broadcast_to(scale[0:1, :], (block, block)).T
        for f in range(feats // 128):
            cols = slice(f * 128, (f + 1) * 128)
            normed_ref[rows, cols] = (combined[rows, cols] * scale * gain[:, cols]).astype(
                jnp.bfloat16
            )

    @pl.loop(0, 2 * nz)
    def _(i):
        c_copy(i).wait_send()

    @pl.loop(0, nz)
    def _(j):
        y_copy(j).wait_send()

    @pl.loop(0, nz - 1)
    def _(j):
        z_copy(j).wait_send()

    @pl.loop(1, n)
    def _(k):
        s_copy(k).wait_send()


def body(n, gate_pre, up_pre, down_weight, residual, norm_gain):
    nz = n // 4
    tokens, depth = gate_pre.shape
    feats = residual.shape[1]
    bf16, f32 = jnp.bfloat16, jnp.float32
    dma = pltpu.SemaphoreType.DMA
    vmem = pl.BlockSpec(memory_space=pltpu.VMEM)
    hbm = pl.BlockSpec(memory_space=pl.ANY)
    out = jax.ShapeDtypeStruct((tokens, feats), bf16)
    return pl.pallas_call(
        functools.partial(kernel, n, down_weight.shape[1]),
        out_shape=(out, out),
        in_specs=[hbm, hbm, hbm, vmem, vmem],
        out_specs=(vmem, vmem),
        scratch_shapes=[
            pltpu.VMEM((tokens, depth), bf16),
            pltpu.VMEM((tokens, depth), bf16),
            pltpu.VMEM((tokens, depth), bf16),
            pltpu.VMEM((SLOTS, depth, feats), bf16),
            pltpu.VMEM((tokens, feats), f32),
            pltpu.VMEM((tokens, feats), f32),
            pltpu.VMEM((2 * nz, tokens, feats), bf16),
            pltpu.VMEM((2 * nz, tokens, feats), bf16),
            pltpu.VMEM((nz, tokens, feats), bf16),
            pltpu.VMEM((nz, tokens, feats), bf16),
            pltpu.VMEM((nz - 1, tokens, feats), bf16),
            pltpu.VMEM((nz - 1, tokens, feats), bf16),
            pltpu.VMEM((n, 8, tokens), f32),
            dma((2, LOADS)),
            dma((SLOTS,)),
            dma((2 * nz,)),
            dma((2 * nz,)),
            dma((nz,)),
            dma((nz,)),
            dma((nz - 1,)),
            dma((nz - 1,)),
            dma((n,)),
            dma((n,)),
        ],
        compiler_params=pltpu.CompilerParams(
            collective_id=0, has_side_effects=True, vmem_limit_bytes=56 * 2**20
        ),
        cost_estimate=pl.CostEstimate(
            flops=2 * tokens * depth * down_weight.shape[1],
            bytes_accessed=2 * depth * (down_weight.shape[1] + 2 * tokens),
            transcendentals=tokens * depth,
        ),
    )(gate_pre, up_pre, down_weight, residual, norm_gain.reshape(1, feats))


def solution(mesh):
    return jax.shard_map(
        functools.partial(body, mesh.shape["hid"]),
        mesh=mesh,
        in_specs=(
            P("groups", "hid"),
            P("groups", "hid"),
            P("hid", None),
            P("groups", "hid"),
            P("hid"),
        ),
        out_specs=(P("groups", "hid"), P("groups", "hid")),
        check_vma=False,
    )
```

time: 268 us -> 90.3 us (0.34)
  waiting for transfers between devices: 181 us -> 0 us
  Pallas kernels: 0 us -> 84.4 us
  matrix products: 37 us -> 0 us
  blocking collectives: 31.5 us -> 0 us
  between operations: 14 us -> 0.64 us
  local copies, waits for them, and re-layouts: 0.66 us -> 5 us
  other arithmetic: 3.82 us -> 0 us
    reduce_scatter x1 -> x0, waiting for transfers between devices: 181 us -> none  [body(): lax.psum_scatter(lax.dot_general(down_weight, hidden, (((0,), (1,)), ((),...]
    pallas_call x0 -> x1, Pallas kernels: none -> 84.4 us  [body(): pl.pallas_call(functools.partial(kernel, n, down_weight.shape[1]), out_sh...]
    dot_general x1 -> x0, matrix products: 37 us -> none  [body(): lax.dot_general(down_weight, hidden, (((0,), (1,)), ((), ())), preferred_...]
    psum x1 -> x0, blocking collectives: 31.5 us -> none  [body(): mean_square = lax.psum(squares, 'hid') / down_weight.shape[1]]
    unnamed x4 -> x2, local copies, waits for them, and re-layouts: 0.66 us -> 3.74 us
  transfers between devices with their start and end apart: 1 -> 0, of which waited for: 1 -> 0; matrix products, arithmetic and copies ran while one was open for 0% -> 0% of each run, Pallas kernels for 0% -> 0%
where the time goes in v1:
time: 90.3 us; the launch traced here: 90.1 us
  Pallas kernels  84.4 us (93%)
  local copies, waits for them, and re-layouts  5 us (6%)
    pallas_call x1, Pallas kernels, body(): pl.pallas_call(functools.partial(kernel, n, down_weight.shape[1]), out_sh...  84.4 us
    unnamed x2, local copies, waits for them, and re-layouts  3.74 us

profile of v1, /device:TPU:0, one launch (start us, length us, event | category | flops | bytes accessed | tf_op | source)
XLA Modules:
  0.0 90.1 jit_solution(3222137897587857924)
XLA Ops:
  0.6 1.3 %reshape.7.gain_ref = bf16[1,512]{1,0:T(2,128)(2,1)} reshape(bf16[512]{0:T(512)(128)(2,1)} %param.9) | data formatting | bytes 2048 | tf_op jit(solution)/shard_map/reshape | solution.py:298
  1.9 84.4 %shard_map.68 = (bf16[512,512]{1,0:T(8,128)(2,1)}, bf16[512,512]{1,0:T(8,128)(2,1)}) custom-call(bf16[512,3072]{1,0:T(8,128)(2,1)} %gate_hbm.1, bf16[512,3072]{1,0:T(8,128)(2,1)} %up_hbm.1, bf16[3072,8192]{1,0:T(8,128)(2,1)} %weight_hbm.1, bf16[512,512]{1,0:T(8,128)(2,1)} %residual_ref.1, bf16[1,512]{1,0:T(2,128)(2,1)} %reshape.7.gain_ref), custom_call_target="tpu_custom_call" | custom-call | flops 25769803776 | bytes 56623104 | tf_op jit(solution)/shard_map/pallas_call | solution.py:260
  86.3 1.9 %copy.9 = bf16[512,512]{1,0:T(8,128)(2,1)} copy(bf16[512,512]{1,0:T(8,128)(2,1)} %get-tuple-element.4) | data formatting | bytes 1048576
  88.2 1.9 %copy.10 = bf16[512,512]{1,0:T(8,128)(2,1)} copy(bf16[512,512]{1,0:T(8,128)(2,1)} %get-tuple-element.5) | data formatting | bytes 1048576

commit v2 on v1

--- a/solution.py
+++ b/solution.py
@@ -14,9 +14,9 @@
 
 def kernel(
     n, total_features,
-    gate_hbm, up_hbm, weight_hbm, residual_ref, gain_ref,
-    stream_ref, normed_ref,
-    gate, up, hidden, weights, acc, combined,
+    gate_hbm, up_hbm, weight_hbm, residual_ref,
+    combined, scale_ref,
+    gate, up, hidden, weights, acc,
     send_c, recv_c, send_y, recv_y, send_z, recv_z, stats,
     load_sem, weight_sem, c_send_sem, c_recv_sem, y_send_sem, y_recv_sem,
     z_send_sem, z_recv_sem, s_send_sem, s_recv_sem,
@@ -54,9 +54,20 @@
         own = s % 2
         return phase, j, own
 
+    below, above = layer, nz - 1 - layer
+    lone = jnp.abs(above - below)
+    both = jnp.minimum(above, below)
+
+    def target(j):
+        m = j - lone
+        alone = jnp.where(above >= below, nz - 1 - j, j)
+        distance = both - m // 2
+        paired = jnp.where(m % 2 == 0, layer + distance, layer - distance)
+        return jnp.where(j < lone, alone, paired)
+
     def weight_copy(s):
         phase, j, own = split(s)
-        dest_z = lax.rem(layer + 1 + j, nz)
+        dest_z = target(j)
         dest_y = jnp.where(phase == 0, 1 - row, row)
         dest_c = jnp.where(own == 1, core, 1 - core)
         dest = (dest_z * 2 + dest_y) * 2 + dest_c
@@ -99,11 +110,20 @@
             device_id={"hid": across}, device_id_type=MESH,
         )
 
-    def z_copy(j):
-        return pltpu.make_async_remote_copy(
-            src_ref=send_z.at[j], dst_ref=recv_z.at[j],
-            send_sem=z_send_sem.at[j], recv_sem=z_recv_sem.at[j],
-            device_id={"hid": lax.rem(me + 4 * (1 + j), n)}, device_id_type=MESH,
+    def z_copy(j, dest):
+        up_way = dest > layer
+        slot = jnp.where(dest == layer - 1, nz, dest)
+        return pltpu.make_async_remote_copy(
+            src_ref=send_z.at[j], dst_ref=recv_z.at[slot],
+            send_sem=z_send_sem.at[j], recv_sem=z_recv_sem.at[slot],
+            device_id={"hid": jnp.where(up_way, me + 4, me - 4)}, device_id_type=MESH,
+        )
+
+    def z_arrival(slot):
+        return pltpu.make_async_remote_copy(
+            src_ref=send_z.at[0], dst_ref=recv_z.at[slot],
+            send_sem=z_send_sem.at[0], recv_sem=z_recv_sem.at[slot],
+            device_id={"hid": sibling}, device_id_type=MESH,
         )
 
     chunk = 64
@@ -155,36 +175,59 @@
             def _():
                 y_copy(j).wait_recv()
 
+                def base(rows):
+                    return (
+                        acc[rows, :] + recv_c[at, rows, :].astype(f32)
+                        + recv_y[j, rows, :].astype(f32)
+                    )
+
                 @pl.when(j < nz - 1)
                 def _():
-                    def work(rows):
-                        send_z[j, rows, :] = (
-                            acc[rows, :] + recv_c[at, rows, :].astype(f32)
-                            + recv_y[j, rows, :].astype(f32)
-                        ).astype(jnp.bfloat16)
-
-                    by_rows(work)
-                    z_copy(j).start()
+                    dest = target(j)
+                    first = jnp.where(dest > layer, layer == 0, layer == nz - 1)
+
+                    @pl.when(first)
+                    def _():
+                        def work(rows):
+                            send_z[j, rows, :] = base(rows).astype(jnp.bfloat16)
+
+                        by_rows(work)
+
+                    @pl.when(jnp.logical_not(first))
+                    def _():
+                        z_arrival(dest).wait_recv()
+
+                        def work(rows):
+                            send_z[j, rows, :] = (
+                                base(rows) + recv_z[dest, rows, :].astype(f32)
+                            ).astype(jnp.bfloat16)
+
+                        by_rows(work)
+
+                    z_copy(j, dest).start()
 
                 @pl.when(j == nz - 1)
                 def _():
                     def work(rows):
-                        combined[rows, :] = (
-                            acc[rows, :] + recv_c[at, rows, :].astype(f32)
-                            + recv_y[j, rows, :].astype(f32)
-                            + residual_ref[rows, :].astype(f32)
-                        )
+                        combined[rows, :] = base(rows) + residual_ref[rows, :].astype(f32)
 
                     by_rows(work)
 
-    @pl.loop(0, nz - 1)
-    def _(j):
-        z_copy(j).wait_recv()
+    def add_arrival(slot):
+        z_arrival(slot).wait_recv()
 
         def work(rows):
-            combined[rows, :] += recv_z[j, rows, :].astype(f32)
+            combined[rows, :] += recv_z[slot, rows, :].astype(f32)
 
         by_rows(work)
+
+    @pl.when(layer > 0)
+    def _():
+        add_arrival(layer)
+
+    @pl.when(layer < nz - 1)
+    def _():
+        add_arrival(nz)
 
     block = 128
 
@@ -192,7 +235,6 @@
     def _(r):
         rows = pl.ds(pl.multiple_of(r * block, block), block)
         values = combined[rows, :]
-        stream_ref[rows, :] = values.astype(jnp.bfloat16)
         squares = values * values
         folded = squares[:, 0:128]
         for f in range(1, feats // 128):
@@ -214,8 +256,6 @@
     @pl.loop(1, n)
     def _(k):
         s_copy(k).wait_recv()
-
-    gain = gain_ref[...].astype(f32)
 
     @pl.loop(0, tokens // block)
     def _(r):
@@ -224,12 +264,7 @@
         for k in range(1, n):
             whole += stats[k, :, rows]
         scale = lax.rsqrt(whole / total_features + 1e-05)
-        scale = jnp.broadcast_to(scale[0:1, :], (block, block)).T
-        for f in range(feats // 128):
-            cols = slice(f * 128, (f + 1) * 128)
-            normed_ref[rows, cols] = (combined[rows, cols] * scale * gain[:, cols]).astype(
-                jnp.bfloat16
-            )
+        scale_ref[rows, :] = jnp.broadcast_to(scale[0:1, :], (block, block)).T
 
     @pl.loop(0, 2 * nz)
     def _(i):
@@ -241,7 +276,7 @@
 
     @pl.loop(0, nz - 1)
     def _(j):
-        z_copy(j).wait_send()
+        z_copy(j, target(j)).wait_send()
 
     @pl.loop(1, n)
     def _(k):
@@ -256,11 +291,13 @@
     dma = pltpu.SemaphoreType.DMA
     vmem = pl.BlockSpec(memory_space=pltpu.VMEM)
     hbm = pl.BlockSpec(memory_space=pl.ANY)
-    out = jax.ShapeDtypeStruct((tokens, feats), bf16)
-    return pl.pallas_call(
+    combined, scale = pl.pallas_call(
         functools.partial(kernel, n, down_weight.shape[1]),
-        out_shape=(out, out),
-        in_specs=[hbm, hbm, hbm, vmem, vmem],
+        out_shape=(
+            jax.ShapeDtypeStruct((tokens, feats), f32),
+            jax.ShapeDtypeStruct((tokens, 128), f32),
+        ),
+        in_specs=[hbm, hbm, hbm, vmem],
         out_specs=(vmem, vmem),
         scratch_shapes=[
             pltpu.VMEM((tokens, depth), bf16),
@@ -268,13 +305,12 @@
             pltpu.VMEM((tokens, depth), bf16),
             pltpu.VMEM((SLOTS, depth, feats), bf16),
             pltpu.VMEM((tokens, feats), f32),
-            pltpu.VMEM((tokens, feats), f32),
             pltpu.VMEM((2 * nz, tokens, feats), bf16),
             pltpu.VMEM((2 * nz, tokens, feats), bf16),
             pltpu.VMEM((nz, tokens, feats), bf16),
             pltpu.VMEM((nz, tokens, feats), bf16),
             pltpu.VMEM((nz - 1, tokens, feats), bf16),
-            pltpu.VMEM((nz - 1, tokens, feats), bf16),
+            pltpu.VMEM((nz + 1, tokens, feats), bf16),
             pltpu.VMEM((n, 8, tokens), f32),
             dma((2, LOADS)),
             dma((SLOTS,)),
@@ -283,7 +319,7 @@
             dma((nz,)),
             dma((nz,)),
             dma((nz - 1,)),
-            dma((nz - 1,)),
+            dma((nz + 1,)),
             dma((n,)),
             dma((n,)),
         ],
@@ -295,7 +331,9 @@
             bytes_accessed=2 * depth * (down_weight.shape[1] + 2 * tokens),
             transcendentals=tokens * depth,
         ),
-    )(gate_pre, up_pre, down_weight, residual, norm_gain.reshape(1, feats))
+    )(gate_pre, up_pre, down_weight, residual)
+    normed = combined * scale[:, :1] * norm_gain.astype(f32)
+    return combined.astype(bf16), normed.astype(bf16)
 
 
 def solution(mesh):

time: 90.3 us -> 85.2 us (0.944)
  Pallas kernels: 84.4 us -> 79.9 us
  local copies, waits for them, and re-layouts: 5 us -> 1.09 us
  other arithmetic: 0 us -> 3.36 us
    pallas_call x1, Pallas kernels: 84.4 us -> 79.9 us  [body(): pl.pallas_call(functools.partial(kernel, n, down_weight.shape[1]), out_sh...]
    unnamed x2 -> x0, local copies, waits for them, and re-layouts: 3.74 us -> none
    convert_element_type x0 -> x2, other arithmetic: none -> 3.36 us  [the longest x1 2.68 us: body(): return (combined.astype(bf16), normed.astype(bf16))]
    reshape x1 -> x0, local copies, waits for them, and re-layouts: 1.26 us -> none  [body(): norm_gain.reshape(1, feats)]
    slice x0 -> x1, local copies, waits for them, and re-layouts: none -> 1.09 us  [body(): normed = combined * scale[:, :1] * norm_gain.astype(f32)]
where the time goes in v2:
time: 85.2 us; the launch traced here: 85 us
  Pallas kernels  79.9 us (94%)
  other arithmetic  3.36 us (4%)
  local copies, waits for them, and re-layouts  1.09 us (1%)
    pallas_call x1, Pallas kernels, body(): pl.pallas_call(functools.partial(kernel, n, down_weight.shape[1]), out_sh...  79.9 us
    convert_element_type x1, other arithmetic, body(): return (combined.astype(bf16), normed.astype(bf16))  2.68 us

profile of v2, /device:TPU:0, one launch (start us, length us, event | category | flops | bytes accessed | tf_op | source)
XLA Modules:
  0.0 85.0 jit_solution(12950106342830210705)
XLA Ops:
  0.6 0.7 convert_element_type.10
  1.3 79.9 %shard_map.68 = (f32[512,512]{1,0:T(8,128)}, f32[512,128]{1,0:T(8,128)}) custom-call(bf16[512,3072]{1,0:T(8,128)(2,1)} %gate_hbm.1, bf16[512,3072]{1,0:T(8,128)(2,1)} %up_hbm.1, bf16[3072,8192]{1,0:T(8,128)(2,1)} %weight_hbm.1, bf16[512,512]{1,0:T(8,128)(2,1)} %residual_ref.1), custom_call_target="tpu_custom_call" | custom-call | flops 25769803776 | bytes 56623104 | tf_op jit(solution)/shard_map/pallas_call | solution.py:294
  81.2 1.1 %slice_reduce_fusion = f32[512]{0:T(512)S(1)} fusion(f32[512,128]{1,0:T(8,128)} %get-tuple-element.5), kind=kLoop, calls=%fused_computation.1 | loop fusion | bytes 4096 | tf_op jit(solution)/shard_map/slice | solution.py:335
  82.3 2.7 %multiply_convert_fusion = (bf16[512,512]{1,0:T(8,128)(2,1)}, bf16[512,512]{1,0:T(8,128)(2,1)}) fusion(f32[512,512]{1,0:T(8,128)} %get-tuple-element.4, f32[512]{0:T(512)S(1)} %convert_element_type.10, f32[512]{0:T(512)S(1)} %slice_reduce_fusion), kind=kLoop, calls=%fused_computation | loop fusion | flops 1048576 | bytes 2101248 | tf_op jit(solution)/shard_map/convert_element_type | solution.py:336

commit v3 on v2

--- a/solution.py
+++ b/solution.py
@@ -16,7 +16,7 @@
     n, total_features,
     gate_hbm, up_hbm, weight_hbm, residual_ref,
     combined, scale_ref,
-    gate, up, hidden, weights, acc,
+    gate, up, hidden, weights, acc, kept,
     send_c, recv_c, send_y, recv_y, send_z, recv_z, stats,
     load_sem, weight_sem, c_send_sem, c_recv_sem, y_send_sem, y_recv_sem,
     z_send_sem, z_recv_sem, s_send_sem, s_recv_sem,
@@ -49,8 +49,8 @@
         )
 
     def split(s):
-        phase = s // (2 * nz)
-        j = (s // 2) % nz
+        phase = (s // 2) % 2
+        j = s // 4
         own = s % 2
         return phase, j, own
 
@@ -135,6 +135,41 @@
 
     f32 = jnp.float32
 
+    def base(j, rows):
+        return (
+            kept[j % 2, rows, :] + recv_c[nz + j, rows, :].astype(f32)
+            + recv_y[j, rows, :].astype(f32)
+        )
+
+    def arrive(j):
+        c_copy(nz + j).wait_recv()
+        y_copy(j).wait_recv()
+
+    def pass_on(j):
+        arrive(j)
+        dest = target(j)
+        first = jnp.where(dest > layer, layer == 0, layer == nz - 1)
+
+        @pl.when(first)
+        def _():
+            def work(rows):
+                send_z[j, rows, :] = base(j, rows).astype(jnp.bfloat16)
+
+            by_rows(work)
+
+        @pl.when(jnp.logical_not(first))
+        def _():
+            z_arrival(dest).wait_recv()
+
+            def work(rows):
+                send_z[j, rows, :] = (
+                    base(j, rows) + recv_z[dest, rows, :].astype(f32)
+                ).astype(jnp.bfloat16)
+
+            by_rows(work)
+
+        z_copy(j, dest).start()
+
     @pl.loop(0, steps)
     def _(s):
         phase, j, own = split(s)
@@ -157,61 +192,35 @@
             by_rows(work)
             c_copy(at).start()
 
-        @pl.when(own == 1)
+        @pl.when((own == 1) & (phase == 0))
         def _():
             c_copy(at).wait_recv()
 
-            @pl.when(phase == 0)
+            def work(rows):
+                send_y[j, rows, :] = (
+                    acc[rows, :] + recv_c[at, rows, :].astype(f32)
+                ).astype(jnp.bfloat16)
+
+            by_rows(work)
+            y_copy(j).start()
+
+        @pl.when((own == 1) & (phase == 1))
+        def _():
+            def work(rows):
+                kept[j % 2, rows, :] = acc[rows, :]
+
+            by_rows(work)
+
+            @pl.when(j > 0)
             def _():
-                def work(rows):
-                    send_y[j, rows, :] = (
-                        acc[rows, :] + recv_c[at, rows, :].astype(f32)
-                    ).astype(jnp.bfloat16)
-
-                by_rows(work)
-                y_copy(j).start()
-
-            @pl.when(phase == 1)
-            def _():
-                y_copy(j).wait_recv()
-
-                def base(rows):
-                    return (
-                        acc[rows, :] + recv_c[at, rows, :].astype(f32)
-                        + recv_y[j, rows, :].astype(f32)
-                    )
-
-                @pl.when(j < nz - 1)
-                def _():
-                    dest = target(j)
-                    first = jnp.where(dest > layer, layer == 0, layer == nz - 1)
-
-                    @pl.when(first)
-                    def _():
-                        def work(rows):
-                            send_z[j, rows, :] = base(rows).astype(jnp.bfloat16)
-
-                        by_rows(work)
-
-                    @pl.when(jnp.logical_not(first))
-                    def _():
-                        z_arrival(dest).wait_recv()
-
-                        def work(rows):
-                            send_z[j, rows, :] = (
-                                base(rows) + recv_z[dest, rows, :].astype(f32)
-                            ).astype(jnp.bfloat16)
-
-                        by_rows(work)
-
-                    z_copy(j, dest).start()
-
-                @pl.when(j == nz - 1)
-                def _():
-                    def work(rows):
-                        combined[rows, :] = base(rows) + residual_ref[rows, :].astype(f32)
-
-                    by_rows(work)
+                pass_on(j - 1)
+
+    arrive(nz - 1)
+
+    def last(rows):
+        combined[rows, :] = base(nz - 1, rows) + residual_ref[rows, :].astype(f32)
+
+    by_rows(last)
 
     def add_arrival(slot):
         z_arrival(slot).wait_recv()
@@ -305,6 +314,7 @@
             pltpu.VMEM((tokens, depth), bf16),
             pltpu.VMEM((SLOTS, depth, feats), bf16),
             pltpu.VMEM((tokens, feats), f32),
+            pltpu.VMEM((2, tokens, feats), f32),
             pltpu.VMEM((2 * nz, tokens, feats), bf16),
             pltpu.VMEM((2 * nz, tokens, feats), bf16),
             pltpu.VMEM((nz, tokens, feats), bf16),

time: 85.2 us -> 85.7 us (level)
  no operation moved by 1% of the time
where the time goes in v3:
time: 85.7 us; the launch traced here: 85.4 us
  Pallas kernels  80.4 us (94%)
  other arithmetic  3.36 us (4%)
  local copies, waits for them, and re-layouts  1.09 us (1%)
    pallas_call x1, Pallas kernels, body(): pl.pallas_call(functools.partial(kernel, n, down_weight.shape[1]), out_sh...  80.4 us
    convert_element_type x1, other arithmetic, body(): return (combined.astype(bf16), normed.astype(bf16))  2.68 us

profile of v3, /device:TPU:0, one launch (start us, length us, event | category | flops | bytes accessed | tf_op | source)
XLA Modules:
  0.0 85.4 jit_solution(16480239540379286609)
XLA Ops:
  0.6 0.7 convert_element_type.10
  1.3 80.4 %shard_map.68 = (f32[512,512]{1,0:T(8,128)}, f32[512,128]{1,0:T(8,128)}) custom-call(bf16[512,3072]{1,0:T(8,128)(2,1)} %gate_hbm.1, bf16[512,3072]{1,0:T(8,128)(2,1)} %up_hbm.1, bf16[3072,8192]{1,0:T(8,128)(2,1)} %weight_hbm.1, bf16[512,512]{1,0:T(8,128)(2,1)} %residual_ref.1), custom_call_target="tpu_custom_call" | custom-call | flops 25769803776 | bytes 56623104 | tf_op jit(solution)/shard_map/pallas_call | solution.py:303
  81.7 1.1 %slice_reduce_fusion = f32[512]{0:T(512)S(1)} fusion(f32[512,128]{1,0:T(8,128)} %get-tuple-element.5), kind=kLoop, calls=%fused_computation.1 | loop fusion | bytes 4096 | tf_op jit(solution)/shard_map/slice | solution.py:345
  82.8 2.7 %multiply_convert_fusion = (bf16[512,512]{1,0:T(8,128)(2,1)}, bf16[512,512]{1,0:T(8,128)(2,1)}) fusion(f32[512,512]{1,0:T(8,128)} %get-tuple-element.4, f32[512]{0:T(512)S(1)} %convert_element_type.10, f32[512]{0:T(512)S(1)} %slice_reduce_fusion), kind=kLoop, calls=%fused_computation | loop fusion | flops 1048576 | bytes 2101248 | tf_op jit(solution)/shard_map/convert_element_type | solution.py:346

commit v4 on v3

--- a/solution.py
+++ b/solution.py
@@ -9,6 +9,7 @@
 
 MESH = pl.DeviceIdType.MESH
 SLOTS = 3
+HALVES = 2
 LOADS = 8
 
 
@@ -103,33 +104,40 @@
             device_id={"hid": sibling}, device_id_type=MESH,
         )
 
-    def y_copy(j):
-        return pltpu.make_async_remote_copy(
-            src_ref=send_y.at[j], dst_ref=recv_y.at[j],
-            send_sem=y_send_sem.at[j], recv_sem=y_recv_sem.at[j],
+    half_rows = tokens // HALVES
+
+    def y_copy(j, h):
+        part = pl.ds(h * half_rows, half_rows)
+        return pltpu.make_async_remote_copy(
+            src_ref=send_y.at[j, part], dst_ref=recv_y.at[j, part],
+            send_sem=y_send_sem.at[j, h], recv_sem=y_recv_sem.at[j, h],
             device_id={"hid": across}, device_id_type=MESH,
         )
 
-    def z_copy(j, dest):
+    def z_copy(j, dest, h):
+        part = pl.ds(h * half_rows, half_rows)
         up_way = dest > layer
         slot = jnp.where(dest == layer - 1, nz, dest)
         return pltpu.make_async_remote_copy(
-            src_ref=send_z.at[j], dst_ref=recv_z.at[slot],
-            send_sem=z_send_sem.at[j], recv_sem=z_recv_sem.at[slot],
+            src_ref=send_z.at[j, part], dst_ref=recv_z.at[slot, part],
+            send_sem=z_send_sem.at[j, h], recv_sem=z_recv_sem.at[slot, h],
             device_id={"hid": jnp.where(up_way, me + 4, me - 4)}, device_id_type=MESH,
         )
 
-    def z_arrival(slot):
-        return pltpu.make_async_remote_copy(
-            src_ref=send_z.at[0], dst_ref=recv_z.at[slot],
-            send_sem=z_send_sem.at[0], recv_sem=z_recv_sem.at[slot],
+    def z_arrival(slot, h):
+        part = pl.ds(h * half_rows, half_rows)
+        return pltpu.make_async_remote_copy(
+            src_ref=send_z.at[0, part], dst_ref=recv_z.at[slot, part],
+            send_sem=z_send_sem.at[0, h], recv_sem=z_recv_sem.at[slot, h],
             device_id={"hid": sibling}, device_id_type=MESH,
         )
 
     chunk = 64
 
-    def by_rows(work):
-        @pl.loop(0, tokens // chunk)
+    def by_rows(work, h=None):
+        first, count = (0, tokens) if h is None else (h * half_rows, half_rows)
+
+        @pl.loop(first // chunk, (first + count) // chunk)
         def _(r):
             work(pl.ds(pl.multiple_of(r * chunk, chunk), chunk))
 
@@ -141,12 +149,13 @@
             + recv_y[j, rows, :].astype(f32)
         )
 
-    def arrive(j):
-        c_copy(nz + j).wait_recv()
-        y_copy(j).wait_recv()
-
-    def pass_on(j):
-        arrive(j)
+    def arrive(j, h):
+        if h == 0:
+            c_copy(nz + j).wait_recv()
+        y_copy(j, h).wait_recv()
+
+    def pass_on(j, h):
+        arrive(j, h)
         dest = target(j)
         first = jnp.where(dest > layer, layer == 0, layer == nz - 1)
 
@@ -155,20 +164,20 @@
             def work(rows):
                 send_z[j, rows, :] = base(j, rows).astype(jnp.bfloat16)
 
-            by_rows(work)
+            by_rows(work, h)
 
         @pl.when(jnp.logical_not(first))
         def _():
-            z_arrival(dest).wait_recv()
+            z_arrival(dest, h).wait_recv()
 
             def work(rows):
                 send_z[j, rows, :] = (
                     base(j, rows) + recv_z[dest, rows, :].astype(f32)
                 ).astype(jnp.bfloat16)
 
-            by_rows(work)
-
-        z_copy(j, dest).start()
+            by_rows(work, h)
+
+        z_copy(j, dest, h).start()
 
     @pl.loop(0, steps)
     def _(s):
@@ -201,34 +210,40 @@
                     acc[rows, :] + recv_c[at, rows, :].astype(f32)
                 ).astype(jnp.bfloat16)
 
-            by_rows(work)
-            y_copy(j).start()
-
-        @pl.when((own == 1) & (phase == 1))
-        def _():
-            def work(rows):
-                kept[j % 2, rows, :] = acc[rows, :]
-
-            by_rows(work)
+            for h in range(HALVES):
+                by_rows(work, h)
+                y_copy(j, h).start()
 
             @pl.when(j > 0)
             def _():
-                pass_on(j - 1)
-
-    arrive(nz - 1)
+                pass_on(j - 1, 0)
+
+        @pl.when((own == 1) & (phase == 1))
+        def _():
+            def work(rows):
+                kept[j % 2, rows, :] = acc[rows, :]
+
+            by_rows(work)
+
+            @pl.when(j > 0)
+            def _():
+                pass_on(j - 1, 1)
+
 
     def last(rows):
         combined[rows, :] = base(nz - 1, rows) + residual_ref[rows, :].astype(f32)
 
-    by_rows(last)
+    for h in range(HALVES):
+        arrive(nz - 1, h)
+        by_rows(last, h)
 
     def add_arrival(slot):
-        z_arrival(slot).wait_recv()
-
         def work(rows):
             combined[rows, :] += recv_z[slot, rows, :].astype(f32)
 
-        by_rows(work)
+        for h in range(HALVES):
+            z_arrival(slot, h).wait_recv()
+            by_rows(work, h)
 
     @pl.when(layer > 0)
     def _():
@@ -249,7 +264,7 @@
         for f in range(1, feats // 128):
             folded += squares[:, f * 128:(f + 1) * 128]
         sums = jnp.sum(folded.T, axis=0, keepdims=True)
-        stats[0, :, rows] = jnp.broadcast_to(sums, (8, block))
+        stats[0, :, rows] = sums
 
     def s_copy(k):
         return pltpu.make_async_remote_copy(
@@ -273,7 +288,7 @@
         for k in range(1, n):
             whole += stats[k, :, rows]
         scale = lax.rsqrt(whole / total_features + 1e-05)
-        scale_ref[rows, :] = jnp.broadcast_to(scale[0:1, :], (block, block)).T
+        scale_ref[rows, :] = jnp.broadcast_to(scale, (block, block)).T
 
     @pl.loop(0, 2 * nz)
     def _(i):
@@ -281,11 +296,13 @@
 
     @pl.loop(0, nz)
     def _(j):
-        y_copy(j).wait_send()
+        for h in range(HALVES):
+            y_copy(j, h).wait_send()
 
     @pl.loop(0, nz - 1)
     def _(j):
-        z_copy(j, target(j)).wait_send()
+        for h in range(HALVES):
+            z_copy(j, target(j), h).wait_send()
 
     @pl.loop(1, n)
     def _(k):
@@ -321,15 +338,15 @@
             pltpu.VMEM((nz, tokens, feats), bf16),
             pltpu.VMEM((nz - 1, tokens, feats), bf16),
             pltpu.VMEM((nz + 1, tokens, feats), bf16),
-            pltpu.VMEM((n, 8, tokens), f32),
+            pltpu.VMEM((n, 1, tokens), f32),
             dma((2, LOADS)),
             dma((SLOTS,)),
             dma((2 * nz,)),
             dma((2 * nz,)),
-            dma((nz,)),
-            dma((nz,)),
-            dma((nz - 1,)),
-            dma((nz + 1,)),
+            dma((nz, HALVES)),
+            dma((nz, HALVES)),
+            dma((nz - 1, HALVES)),
+            dma((nz + 1, HALVES)),
             dma((n,)),
             dma((n,)),
         ],

time: 85.7 us -> 74.5 us (0.87)
  Pallas kernels: 80.4 us -> 69.2 us
    pallas_call x1, Pallas kernels: 80.4 us -> 69.2 us  [body(): pl.pallas_call(functools.partial(kernel, n, down_weight.shape[1]), out_sh...]
where the time goes in v4:
time: 74.5 us; the launch traced here: 74.3 us
  Pallas kernels  69.2 us (93%)
  other arithmetic  3.36 us (5%)
  local copies, waits for them, and re-layouts  1.09 us (1%)
    pallas_call x1, Pallas kernels, body(): pl.pallas_call(functools.partial(kernel, n, down_weight.shape[1]), out_sh...  69.2 us
    convert_element_type x1, other arithmetic, body(): return (combined.astype(bf16), normed.astype(bf16))  2.68 us

profile of v4, /device:TPU:0, one launch (start us, length us, event | category | flops | bytes accessed | tf_op | source)
XLA Modules:
  0.0 74.3 jit_solution(9823048185729859345)
XLA Ops:
  0.6 0.7 convert_element_type.10
  1.3 69.2 %shard_map.68 = (f32[512,512]{1,0:T(8,128)}, f32[512,128]{1,0:T(8,128)}) custom-call(bf16[512,3072]{1,0:T(8,128)(2,1)} %gate_hbm.1, bf16[512,3072]{1,0:T(8,128)(2,1)} %up_hbm.1, bf16[3072,8192]{1,0:T(8,128)(2,1)} %weight_hbm.1, bf16[512,512]{1,0:T(8,128)(2,1)} %residual_ref.1), custom_call_target="tpu_custom_call" | custom-call | flops 25769803776 | bytes 56623104 | tf_op jit(solution)/shard_map/pallas_call | solution.py:320
  70.5 1.1 %slice_reduce_fusion = f32[512]{0:T(512)S(1)} fusion(f32[512,128]{1,0:T(8,128)} %get-tuple-element.5), kind=kLoop, calls=%fused_computation.1 | loop fusion | bytes 4096 | tf_op jit(solution)/shard_map/slice | solution.py:362
  71.6 2.7 %multiply_convert_fusion = (bf16[512,512]{1,0:T(8,128)(2,1)}, bf16[512,512]{1,0:T(8,128)(2,1)}) fusion(f32[512,512]{1,0:T(8,128)} %get-tuple-element.4, f32[512]{0:T(512)S(1)} %convert_element_type.10, f32[512]{0:T(512)S(1)} %slice_reduce_fusion), kind=kLoop, calls=%fused_computation | loop fusion | flops 1048576 | bytes 2101248 | tf_op jit(solution)/shard_map/convert_element_type | solution.py:363

commit v5 on v4

--- a/solution.py
+++ b/solution.py
@@ -9,7 +9,7 @@
 
 MESH = pl.DeviceIdType.MESH
 SLOTS = 3
-HALVES = 2
+PIECES = 4
 LOADS = 8
 
 
@@ -104,10 +104,10 @@
             device_id={"hid": sibling}, device_id_type=MESH,
         )
 
-    half_rows = tokens // HALVES
+    piece_rows = tokens // PIECES
 
     def y_copy(j, h):
-        part = pl.ds(h * half_rows, half_rows)
+        part = pl.ds(h * piece_rows, piece_rows)
         return pltpu.make_async_remote_copy(
             src_ref=send_y.at[j, part], dst_ref=recv_y.at[j, part],
             send_sem=y_send_sem.at[j, h], recv_sem=y_recv_sem.at[j, h],
@@ -115,7 +115,7 @@
         )
 
     def z_copy(j, dest, h):
-        part = pl.ds(h * half_rows, half_rows)
+        part = pl.ds(h * piece_rows, piece_rows)
         up_way = dest > layer
         slot = jnp.where(dest == layer - 1, nz, dest)
         return pltpu.make_async_remote_copy(
@@ -125,7 +125,7 @@
         )
 
     def z_arrival(slot, h):
-        part = pl.ds(h * half_rows, half_rows)
+        part = pl.ds(h * piece_rows, piece_rows)
         return pltpu.make_async_remote_copy(
             src_ref=send_z.at[0, part], dst_ref=recv_z.at[slot, part],
             send_sem=z_send_sem.at[0, h], recv_sem=z_recv_sem.at[slot, h],
@@ -135,7 +135,7 @@
     chunk = 64
 
     def by_rows(work, h=None):
-        first, count = (0, tokens) if h is None else (h * half_rows, half_rows)
+        first, count = (0, tokens) if h is None else (h * piece_rows, piece_rows)
 
         @pl.loop(first // chunk, (first + count) // chunk)
         def _(r):
@@ -210,13 +210,14 @@
                     acc[rows, :] + recv_c[at, rows, :].astype(f32)
                 ).astype(jnp.bfloat16)
 
-            for h in range(HALVES):
+            for h in range(PIECES):
                 by_rows(work, h)
                 y_copy(j, h).start()
 
             @pl.when(j > 0)
             def _():
-                pass_on(j - 1, 0)
+                for h in range(PIECES // 2):
+                    pass_on(j - 1, h)
 
         @pl.when((own == 1) & (phase == 1))
         def _():
@@ -227,13 +228,14 @@
 
             @pl.when(j > 0)
             def _():
-                pass_on(j - 1, 1)
+                for h in range(PIECES // 2, PIECES):
+                    pass_on(j - 1, h)
 
 
     def last(rows):
         combined[rows, :] = base(nz - 1, rows) + residual_ref[rows, :].astype(f32)
 
-    for h in range(HALVES):
+    for h in range(PIECES):
         arrive(nz - 1, h)
         by_rows(last, h)
 
@@ -241,7 +243,7 @@
         def work(rows):
             combined[rows, :] += recv_z[slot, rows, :].astype(f32)
 
-        for h in range(HALVES):
+        for h in range(PIECES):
             z_arrival(slot, h).wait_recv()
             by_rows(work, h)
 
@@ -296,12 +298,12 @@
 
     @pl.loop(0, nz)
     def _(j):
-        for h in range(HALVES):
+        for h in range(PIECES):
             y_copy(j, h).wait_send()
 
     @pl.loop(0, nz - 1)
     def _(j):
-        for h in range(HALVES):
+        for h in range(PIECES):
             z_copy(j, target(j), h).wait_send()
 
     @pl.loop(1, n)
@@ -343,10 +345,10 @@
             dma((SLOTS,)),
             dma((2 * nz,)),
             dma((2 * nz,)),
-            dma((nz, HALVES)),
-            dma((nz, HALVES)),
-            dma((nz - 1, HALVES)),
-            dma((nz + 1, HALVES)),
+            dma((nz, PIECES)),
+            dma((nz, PIECES)),
+            dma((nz - 1, PIECES)),
+            dma((nz + 1, PIECES)),
             dma((n,)),
             dma((n,)),
         ],

time: 74.5 us -> 74.6 us (level)
  no operation moved by 1% of the time
where the time goes in v5:
time: 74.6 us; the launch traced here: 74.4 us
  Pallas kernels  69.3 us (93%)
  other arithmetic  3.36 us (5%)
  local copies, waits for them, and re-layouts  1.09 us (1%)
    pallas_call x1, Pallas kernels, body(): pl.pallas_call(functools.partial(kernel, n, down_weight.shape[1]), out_sh...  69.3 us
    convert_element_type x1, other arithmetic, body(): return (combined.astype(bf16), normed.astype(bf16))  2.68 us

profile of v5, /device:TPU:0, one launch (start us, length us, event | category | flops | bytes accessed | tf_op | source)
XLA Modules:
  0.0 74.4 jit_solution(2266647357510017788)
XLA Ops:
  0.6 0.7 convert_element_type.10
  1.3 69.3 %shard_map.68 = (f32[512,512]{1,0:T(8,128)}, f32[512,128]{1,0:T(8,128)}) custom-call(bf16[512,3072]{1,0:T(8,128)(2,1)} %gate_hbm.1, bf16[512,3072]{1,0:T(8,128)(2,1)} %up_hbm.1, bf16[3072,8192]{1,0:T(8,128)(2,1)} %weight_hbm.1, bf16[512,512]{1,0:T(8,128)(2,1)} %residual_ref.1), custom_call_target="tpu_custom_call" | custom-call | flops 25769803776 | bytes 56623104 | tf_op jit(solution)/shard_map/pallas_call | solution.py:322
  70.6 1.1 %slice_reduce_fusion = f32[512]{0:T(512)S(1)} fusion(f32[512,128]{1,0:T(8,128)} %get-tuple-element.5), kind=kLoop, calls=%fused_computation.1 | loop fusion | bytes 4096 | tf_op jit(solution)/shard_map/slice | solution.py:364
  71.7 2.7 %multiply_convert_fusion = (bf16[512,512]{1,0:T(8,128)(2,1)}, bf16[512,512]{1,0:T(8,128)(2,1)}) fusion(f32[512,512]{1,0:T(8,128)} %get-tuple-element.4, f32[512]{0:T(512)S(1)} %convert_element_type.10, f32[512]{0:T(512)S(1)} %slice_reduce_fusion), kind=kLoop, calls=%fused_computation | loop fusion | flops 1048576 | bytes 2101248 | tf_op jit(solution)/shard_map/convert_element_type | solution.py:365
